TPU v7x, 512 devices: a whole 4x8x8 slice. The times are simulated.
512 devices in a mesh: section: 8 (over y), expert: 64 (over x, z, core).
Axes of the slice: x: 4, y: 8, z: 8, core: 2. Of those that a mesh axis runs over, the one named last changes fastest.
Arguments:
- layer_input: bfloat16 [8, 4096, 2048], P('section', 'expert'), may hold values from -6 to 6
- out_grad: bfloat16 [8, 4096, 2048], P('section', 'expert'), may hold values from -6 to 6
- norm_gain: float32 [8, 2048], P('section'), may hold values from 0.5 to 1.5
- expert_ids: int32 [8, 4096, 8], P('section', 'expert'), may hold values from 0 to 127, all different within a row; in each aligned block of 64 rows (0 to 63, 64 to 127, ..., all dimensions but the last counted through in order) at most 8 rows name the same one
- combine: bfloat16 [8, 4096, 8], P('section', 'expert'), may hold values from 0.049804688 to 0.29882812
- w_gate: bfloat16 [8, 12288, 2048], P('section', 'expert'), may hold values from -0.125 to 0.125
- w_up: bfloat16 [8, 12288, 2048], P('section', 'expert'), may hold values from -0.125 to 0.125
- w_down: bfloat16 [8, 12288, 2048], P('section', 'expert'), may hold values from -0.21875 to 0.21875
Outputs:
- passed_grad: bfloat16 [8, 4096, 2048], P('section', 'expert')
- comb_grad: bfloat16 [8, 4096, 8], P('section', 'expert')
- gain_grad: float32 [8, 2048], P('section')
Inputs may be any that keep to these rules, and one draw needn't show every extreme that they name: `expert_ids`: A token names 8 different experts. Within the tokens of one device (aligned blocks of 64 tokens of a section) no expert is named by more than 8 tokens, a bound that some block reaches.
All inputs are finite; a program needn't handle non-finite values.
Results may differ from a plain program's by a relative error of at most 0.0075.
Values may be sent and summed in bfloat16 or wider, within the bound.
A program may use at most 64 MiB of HBM per device.

v0:
```python
import jax
import jax.numpy as jnp
from jax import lax
from jax.sharding import PartitionSpec as P

EXPERTS = 16
CAP = 8


epsilon = 1e-06


def from_behind(block, axis, distance):
    devices = range(lax.axis_size(axis))
    route = [(i - distance, i) for i in devices if i - distance in devices]
    return lax.ppermute(block, axis, route)


def contract_cols(left, right):
    return lax.dot_general(
        left, right, (((1,), (1,)), ((), ())), preferred_element_type=jnp.float32
    )


def exact_rows(left, right):
    return lax.dot_general(
        left,
        right,
        (((0,), (0,)), ((), ())),
        preferred_element_type=jnp.float32,
        precision=lax.Precision.HIGHEST,
    )


def forward_part(rows_x, weight_gate, weight_up, weight_down):
    gate = contract_cols(rows_x, weight_gate)
    upper = contract_cols(rows_x, weight_up)
    sigma = jax.nn.sigmoid(gate)
    active = gate * sigma
    hidden = (active * upper).astype(jnp.bfloat16)
    output = jnp.dot(hidden, weight_down, preferred_element_type=jnp.float32)
    return (gate, upper, sigma, active, hidden, output)


def backward_part(rows_dy, rows_w, early, weight_gate, weight_up, weight_down):
    gate, upper, sigma, active, hidden, output = early
    comb_part = jnp.sum(rows_dy.astype(jnp.float32) * output, axis=-1).astype(jnp.bfloat16)
    scaled = (rows_w.astype(jnp.float32)[:, None] * rows_dy.astype(jnp.float32)).astype(
        jnp.bfloat16
    )
    hidden_grad = contract_cols(scaled, weight_down)
    gate_part = (hidden_grad * upper * sigma * (1.0 + gate * (1.0 - sigma))).astype(jnp.bfloat16)
    up_part = (hidden_grad * active).astype(jnp.bfloat16)
    rows_grad = (
        jnp.dot(gate_part, weight_gate, preferred_element_type=jnp.float32)
        + jnp.dot(up_part, weight_up, preferred_element_type=jnp.float32)
    ).astype(jnp.bfloat16)
    return (rows_grad, comb_part)


def per_device(layer_input, out_grad, norm_gain, expert_ids, combine, w_gate, w_up, w_down):
    inputs = layer_input[0]
    incoming_gradient = out_grad[0]
    scale_factors = norm_gain[0]
    choices = expert_ids[0]
    weights = combine[0]
    weight_gate = w_gate[0]
    weight_up = w_up[0]
    weight_down = w_down[0]
    tokens_here, width = inputs.shape
    top_count = choices.shape[1]
    peers = lax.axis_size("expert")
    sharing = peers // EXPERTS
    route_count = tokens_here * top_count
    slot_total = EXPERTS * CAP
    peer_slots = peers * CAP
    float_values = inputs.astype(jnp.float32)
    reciprocal_norm = lax.rsqrt(
        jnp.mean(float_values * float_values, axis=-1, keepdims=True) + epsilon
    )
    normalized_rows = float_values * reciprocal_norm
    normalized_input = (normalized_rows * scale_factors[None, :]).astype(jnp.bfloat16)
    flat_ids = choices.reshape(route_count)
    onehot = (flat_ids[:, None] == jnp.arange(EXPERTS, dtype=jnp.int32)[None, :]).astype(jnp.int32)
    before = jnp.cumsum(onehot, axis=0) - onehot
    slot = jnp.sum(before * onehot, axis=1)
    target = flat_ids * CAP + slot
    route_pick = (target[None, :] == jnp.arange(slot_total, dtype=jnp.int32)[:, None]).astype(
        jnp.bfloat16
    )
    token_pick = jnp.sum(route_pick.reshape(slot_total, tokens_here, top_count), axis=-1)
    send_x = jnp.dot(token_pick, normalized_input, preferred_element_type=jnp.float32).astype(
        jnp.bfloat16
    )
    send_x = jnp.repeat(send_x.reshape(EXPERTS, CAP, width), sharing, axis=0)
    send_dy = jnp.dot(token_pick, incoming_gradient, preferred_element_type=jnp.float32).astype(
        jnp.bfloat16
    )
    send_dy = jnp.repeat(send_dy.reshape(EXPERTS, CAP, width), sharing, axis=0)
    send_w = jnp.dot(
        route_pick, weights.reshape(route_count, 1), preferred_element_type=jnp.float32
    )
    send_w = jnp.repeat(send_w.astype(jnp.bfloat16).reshape(EXPERTS, CAP), sharing, axis=0)
    early = None
    rows_x, rows_dy, rows_w = (
        lax.all_to_all(send_x, "expert", split_axis=0, concat_axis=0, tiled=True),
        lax.all_to_all(send_dy, "expert", split_axis=0, concat_axis=0, tiled=True),
        lax.all_to_all(send_w, "expert", split_axis=0, concat_axis=0, tiled=True),
    )
    flat_rows = rows_x.reshape(peer_slots, width)
    early = forward_part(flat_rows, weight_gate, weight_up, weight_down)
    rows_grad, comb_part = backward_part(
        rows_dy.reshape(peer_slots, width),
        rows_w.reshape(peer_slots),
        early,
        weight_gate,
        weight_up,
        weight_down,
    )
    back_rows, back_comb = (
        lax.all_to_all(
            rows_grad.reshape(peers, CAP, width), "expert", split_axis=0, concat_axis=0, tiled=True
        ),
        lax.all_to_all(
            comb_part.reshape(peers, CAP), "expert", split_axis=0, concat_axis=0, tiled=True
        ),
    )
    summed_rows = jnp.sum(
        back_rows.reshape(EXPERTS, sharing, CAP, width).astype(jnp.float32), axis=1
    )
    summed_comb = jnp.sum(back_comb.reshape(EXPERTS, sharing, CAP).astype(jnp.float32), axis=1)
    normalized_gradient = exact_rows(
        token_pick.astype(jnp.float32), summed_rows.reshape(slot_total, width)
    )
    comb_out = exact_rows(route_pick.astype(jnp.float32), summed_comb.reshape(slot_total, 1))
    comb_out = comb_out.astype(jnp.bfloat16).reshape(tokens_here, top_count)
    gain_correction = jnp.sum(normalized_gradient * normalized_rows, axis=0)
    scaled_gradient = normalized_gradient * scale_factors[None, :]
    inner_product = jnp.mean(scaled_gradient * normalized_rows, axis=-1, keepdims=True)
    input_gradient = (
        incoming_gradient.astype(jnp.float32)
        + reciprocal_norm * (scaled_gradient - normalized_rows * inner_product)
    ).astype(jnp.bfloat16)
    passed = from_behind(input_gradient, "section", -1)
    gain_total = lax.psum(gain_correction, "expert")
    return (passed[None], comb_out[None], gain_total[None])


def solution(mesh):
    placed = (
        P("section", "expert", None),
        P("section", "expert", None),
        P("section", None),
        P("section", "expert", None),
        P("section", "expert", None),
        P("section", "expert", None),
        P("section", "expert", None),
        P("section", "expert", None),
    )
    return jax.shard_map(
        per_device,
        mesh=mesh,
        in_specs=placed,
        out_specs=(P("section", "expert", None), P("section", "expert", None), P("section", None)),
        check_vma=False,
    )
```

profile of v0, /device:TPU:56, one launch (start us, length us, event | category | flops | bytes accessed | tf_op | source)
XLA Modules:
  0.0 356.8 jit_solution(8759035831997450475)
XLA Ops:
  0.6 0.8 copy.33
  1.7 0.8 copy.37
  2.6 1.2 reduce-window.6
  5.0 13.8 %all-to-all-start = ((bf16[64,1,8]{2,1,0:T(2,128)(2,1)}), bf16[64,1,8]{2,1,0:T(2,128)(2,1)S(1)}, u32[]{:S(2)}, u32[]{:S(2)}) async-start(bf16[64,1,8]{2,1,0:T(2,128)(2,1)} %copy.38), calls=%async_computation | async-start | bytes 65536 | tf_op jit(solution)/shard_map/all_to_all | solution.py:108
  18.9 1.1 fusion.35
  20.2 1.3 fusion.5
  21.5 6.7 %all-to-all-done = bf16[64,1,8]{2,1,0:T(2,128)(2,1)S(1)} async-done(((bf16[64,1,8]{2,1,0:T(2,128)(2,1)}), bf16[64,1,8]{2,1,0:T(2,128)(2,1)S(1)}, u32[]{:S(2)}, u32[]{:S(2)}) %all-to-all-start) | async-done | bytes 1056 | tf_op jit(solution)/shard_map/all_to_all | solution.py:108
  28.2 1.6 broadcast_in_dim.23
  29.9 4.7 %all-to-all-start.2 = ((bf16[64,8,2048]{2,1,0:T(8,128)(2,1)}), bf16[64,8,2048]{2,1,0:T(8,128)(2,1)S(1)}, u32[]{:S(2)}, u32[]{:S(2)}) async-start(bf16[64,8,2048]{2,1,0:T(8,128)(2,1)} %bitcast.14), calls=%async_computation.2 | async-start | bytes 4194304 | tf_op jit(solution)/shard_map/all_to_all | solution.py:106
  34.6 1.3 fusion.4
  35.8 49.9 %all-to-all-done.2 = bf16[64,8,2048]{2,1,0:T(8,128)(2,1)S(1)} async-done(((bf16[64,8,2048]{2,1,0:T(8,128)(2,1)}), bf16[64,8,2048]{2,1,0:T(8,128)(2,1)S(1)}, u32[]{:S(2)}, u32[]{:S(2)}) %all-to-all-start.2) | async-done | bytes 2097184 | tf_op jit(solution)/shard_map/all_to_all | solution.py:106
  85.7 1.8 broadcast_in_dim.22
  87.7 5.9 %all-to-all-start.1 = ((bf16[64,8,2048]{2,1,0:T(8,128)(2,1)}), bf16[64,8,2048]{2,1,0:T(8,128)(2,1)S(1)}, u32[]{:S(2)}, u32[]{:S(2)}) async-start(bf16[64,8,2048]{2,1,0:T(8,128)(2,1)} %bitcast.8), calls=%async_computation.1 | async-start | bytes 4194304 | tf_op jit(solution)/shard_map/all_to_all | solution.py:107
  93.7 2.6 fusion.9
  96.3 1.6 fusion.11
  97.9 46.9 %all-to-all-done.1 = bf16[64,8,2048]{2,1,0:T(8,128)(2,1)S(1)} async-done(((bf16[64,8,2048]{2,1,0:T(8,128)(2,1)}), bf16[64,8,2048]{2,1,0:T(8,128)(2,1)S(1)}, u32[]{:S(2)}, u32[]{:S(2)}) %all-to-all-start.1) | async-done | bytes 2097184 | tf_op jit(solution)/shard_map/all_to_all | solution.py:107
  144.8 2.1 fusion.7
  146.9 0.8 fusion.17
  148.8 56.9 %all_to_all.30 = bf16[64,8,2048]{2,1,0:T(8,128)(2,1)S(1)} all-to-all(bf16[64,8,2048]{2,1,0:T(8,128)(2,1)S(1)} %fusion.3), channel_id=1, replica_groups=mesh['section'=8,'expert'=64] {'expert'}, dimensions={0} | all-to-all | bytes 4194304 | tf_op jit(solution)/shard_map/all_to_all | solution.py:121
  207.4 0.9 fusion.33
  208.3 3.3 collective-permute-start
  211.6 0.9 fusion.2
  212.6 15.2 %all_to_all.31 = bf16[64,1,8]{2,1,0:T(2,128)(2,1)S(1)} all-to-all(bf16[64,1,8]{2,1,0:T(2,128)(2,1)S(1)} %convert_element_type.145), channel_id=1, replica_groups=mesh['section'=8,'expert'=64] {'expert'}, dimensions={0} | all-to-all | bytes 2048 | tf_op jit(solution)/shard_map/all_to_all | solution.py:124
  228.9 127.2 %psum.7 = f32[1,2048]{1,0:T(1,128)} all-reduce(f32[1,2048]{1,0:T(1,128)S(1)} %bitcast.102), channel_id=1, replica_groups=mesh['section'=8,'expert'=64] {'expert'}, use_global_device_ids=true, to_apply=%region_10.11 | all-reduce | flops 2048 | bytes 16384 | tf_op jit(solution)/shard_map/psum | solution.py:145
  (52 shorter events, 6.7 us)
Async XLA Ops:
  0.6 93.0 %copy-start = (bf16[1,192,2048]{2,1,0:T(8,128)(2,1)S(1)}, bf16[1,192,2048]{2,1,0:T(8,128)(2,1)}, u32[]{:S(2)}) copy-start(bf16[1,192,2048]{2,1,0:T(8,128)(2,1)} %param.13) | copy-start | bytes 2359300
  5.0 23.2 %all-to-all-start = ((bf16[64,1,8]{2,1,0:T(2,128)(2,1)}), bf16[64,1,8]{2,1,0:T(2,128)(2,1)S(1)}, u32[]{:S(2)}, u32[]{:S(2)}) async-start(bf16[64,1,8]{2,1,0:T(2,128)(2,1)} %copy.38), calls=%async_computation | async-start | bytes 65536 | tf_op jit(solution)/shard_map/all_to_all | solution.py:108
  29.9 55.9 %all-to-all-start.2 = ((bf16[64,8,2048]{2,1,0:T(8,128)(2,1)}), bf16[64,8,2048]{2,1,0:T(8,128)(2,1)S(1)}, u32[]{:S(2)}, u32[]{:S(2)}) async-start(bf16[64,8,2048]{2,1,0:T(8,128)(2,1)} %bitcast.14), calls=%async_computation.2 | async-start | bytes 4194304 | tf_op jit(solution)/shard_map/all_to_all | solution.py:106
  85.7 2.0 copy-start.2
  87.7 57.1 %all-to-all-start.1 = ((bf16[64,8,2048]{2,1,0:T(8,128)(2,1)}), bf16[64,8,2048]{2,1,0:T(8,128)(2,1)S(1)}, u32[]{:S(2)}, u32[]{:S(2)}) async-start(bf16[64,8,2048]{2,1,0:T(8,128)(2,1)} %bitcast.8), calls=%async_computation.1 | async-start | bytes 4194304 | tf_op jit(solution)/shard_map/all_to_all | solution.py:107
  93.7 2.6 copy-start.3
  93.7 2.6 copy-start.5
  144.8 2.1 copy-start.7
  146.9 1.1 copy-start.6
  205.7 1.0 copy-start.1
  205.7 1.0 copy-start.8
  205.7 1.7 copy-start.4
  206.6 4.9 %copy-start.9 = (bf16[1,192,2048]{2,1,0:T(8,128)(2,1)S(1)}, bf16[1,192,2048]{2,1,0:T(8,128)(2,1)}, u32[]{:S(2)}) copy-start(bf16[1,192,2048]{2,1,0:T(8,128)(2,1)} %param.15) | copy-start | bytes 2359300
  208.3 147.8 %collective-permute-start = (bf16[64,2048]{1,0:T(8,128)(2,1)}, bf16[64,2048]{1,0:T(8,128)(2,1)S(1)}, u32[]{:S(2)}, u32[]{:S(2)}) collective-permute-start(bf16[64,2048]{1,0:T(8,128)(2,1)} %fusion.33), channel_id=1, source_target_pairs={{64,0},{128,64},{192,128},{256,192},{320,256},{384,320},{448,384},... | collective-permute-start | bytes 786440 | tf_op jit(solution)/shard_map/ppermute | solution.py:16
where the time goes:
time: 357 us
  blocking collectives  199 us (56%)
  waiting for transfers between devices  104 us (29%)
  starting transfers between devices  27.6 us (8%)
  matrix products  12.4 us (3%)
  local copies, waits for them, and re-layouts  9.12 us (3%)
  other arithmetic  3.98 us (1%)
    psum x1, blocking collectives, per_device(): gain_total = lax.psum(gain_correction, 'expert')  127 us
    all_to_all x1, blocking collectives, per_device(): lax.all_to_all(rows_grad.reshape(peers, CAP, width), 'expert', split_axis...  56.9 us
    all_to_all x1, waiting for transfers between devices, per_device(): lax.all_to_all(send_x, 'expert', split_axis=0, concat_axis=0, tiled=True)  49.9 us
    all_to_all x1, waiting for transfers between devices, per_device(): lax.all_to_all(send_dy, 'expert', split_axis=0, concat_axis=0, tiled=True)  46.9 us
    all_to_all x1, blocking collectives, per_device(): lax.all_to_all(comb_part.reshape(peers, CAP), 'expert', split_axis=0, con...  15.2 us
    all_to_all x1, starting transfers between devices, per_device(): lax.all_to_all(send_w, 'expert', split_axis=0, concat_axis=0, tiled=True)  13.8 us
  transfers between devices with their start and end apart: 4, of which 3 were waited for; matrix products, arithmetic and copies ran while one was open for 3% of the time, Pallas kernels for 0%

commit v1 on v0

v1 whole, which is shorter than its diff:
```python
import jax
import jax.numpy as jnp
from jax import lax
from jax.experimental import pallas as pl
from jax.experimental.pallas import tpu as pltpu
from jax.sharding import PartitionSpec as P

MESH = pl.DeviceIdType.MESH
NX, NZ = 4, 8
CAP = 8
D = 2048
HALF = D // 2
HID = 192
TOK = 64
TOP = 8
BACK = HALF + 128
EPS = 1e-06
F32, BF16 = jnp.float32, jnp.bfloat16


def nt(left, right):
    return lax.dot_general(left, right, (((1,), (1,)), ((), ())), preferred_element_type=F32)


def nn(left, right):
    return jnp.dot(left, right, preferred_element_type=F32)


def kernel(
    x_ref, dy_ref, g_ref, ids_ref, cw_ref, wg_ref, wu_ref, wd_ref,
    passed_ref, comb_ref, gain_ref,
    send, recv, w, ret, got, grads, sum_xc, sum_z,
    disp_sem, recv_sem, fwd_sem, ret_sem, got_sem, wl_sem, ws_sem, wr_sem,
    xs_sem, xr_sem, zs_sem, zr_sem, pass_sem,
):
    sec = lax.axis_index("section")
    me = lax.axis_index("expert")
    core = lax.rem(me, 2)
    z = lax.rem(me // 2, NZ)
    x = me // (2 * NZ)
    way = 1 - 2 * lax.rem(z, 2)
    mate_z = z + way

    def place(px, pz, pc):
        return (sec, (lax.rem(px + NX, NX) * NZ + lax.rem(pz + 2 * NZ, NZ)) * 2 + pc)

    def entry_z(d):
        return z + way * d if d % 2 == 0 else z - way * d

    sibling = place(x, z, 1 - core)
    mate = place(x, mate_z, core)
    ahead = (lax.rem(sec + 7, 8), me)
    behind = (lax.rem(sec + 1, 8), me)

    barrier = pltpu.get_barrier_semaphore()

    def greet(q, carry):
        chip = lax.rem(x * NZ + z + q, NX * NZ)
        pl.semaphore_signal(barrier, inc=1, device_id=(sec, chip * 2 + core), device_id_type=MESH)
        return carry

    lax.fori_loop(1, NX * NZ, greet, 0)
    for q in range(NX):
        pl.semaphore_signal(
            barrier, inc=1, device_id=place(x + q, z, 1 - core), device_id_type=MESH
        )
    for other in (ahead, behind):
        pl.semaphore_signal(barrier, inc=1, device_id=other, device_id_type=MESH)

    own = []
    for n, ref in enumerate((wg_ref, wu_ref, wd_ref)):
        copy = pltpu.make_async_copy(ref, w.at[2 * n], wl_sem.at[n])
        copy.start()
        own.append(copy)

    rows = x_ref[...].astype(F32)
    rinv = lax.rsqrt(jnp.mean(rows * rows, axis=-1, keepdims=True) + EPS)
    normed = (rows * rinv * g_ref[...]).astype(BF16)
    dy = dy_ref[...]
    ids = ids_ref[...]
    weights = cw_ref[...].astype(F32)

    def expert_of(block):
        d, dx = block // 4, lax.rem(block, 4)
        ez = jnp.where(lax.rem(d, 2) == 0, z + way * d, z - way * d)
        ez = lax.rem(ez + 2 * NZ, NZ)
        return lax.rem(x + dx, NX) * 4 + ez // 2

    before = (
        lax.broadcasted_iota(jnp.int32, (TOK, TOK), 0)
        > lax.broadcasted_iota(jnp.int32, (TOK, TOK), 1)
    ).astype(BF16)

    def picks(lanes, per):
        lane = lax.broadcasted_iota(jnp.int32, (TOK, lanes), 1)
        expert = expert_of(lane // per)
        named = jnp.zeros((TOK, lanes), F32)
        scaled = jnp.zeros((TOK, lanes), F32)
        for k in range(TOP):
            hit = ids[:, k : k + 1] == expert
            named = jnp.where(hit, 1.0, named)
            scaled = jnp.where(hit, weights[:, k : k + 1], scaled)
        rank = nn(before, named.astype(BF16))
        mine = rank == lax.rem(lane, CAP).astype(F32)
        return lane, expert, jnp.where(mine, named, 0.0), jnp.where(mine, scaled, 0.0)

    _, _, token_pick, _ = picks(128, CAP)
    pick = token_pick.astype(BF16)

    def tn(left, right):
        return lax.dot_general(left, right, (((0,), (0,)), ((), ())), preferred_element_type=F32)

    for c in range(4):
        cols = slice(c * 512, (c + 1) * 512)
        part_x = tn(pick, normed[:, cols]).reshape(16, CAP, 512)
        part_dy = tn(pick, dy[:, cols]).reshape(16, CAP, 512)
        send[:, :, cols] = jnp.concatenate([part_x, part_dy], axis=1).astype(BF16)
    recv[0, 0] = send[0]

    pl.semaphore_wait(barrier, NX * NZ - 1 + NX + 2)

    def dispatch(d, dx):
        return pltpu.make_async_remote_copy(
            src_ref=send.at[d * 4 + dx],
            dst_ref=recv.at[d, dx],
            send_sem=disp_sem.at[d * 4 + dx],
            recv_sem=recv_sem.at[d * 4 + dx],
            device_id=place(x + dx, entry_z(d), core),
            device_id_type=MESH,
        )

    def hand_on(d, dx):
        return pltpu.make_async_remote_copy(
            src_ref=recv.at[d, dx],
            dst_ref=recv.at[d + 4, dx],
            send_sem=fwd_sem.at[d * 4 + dx],
            recv_sem=recv_sem.at[16 + d * 4 + dx],
            device_id=mate,
            device_id_type=MESH,
        )

    def weight_swap(n, ref):
        return pltpu.make_async_remote_copy(
            src_ref=ref,
            dst_ref=w.at[2 * n + 1],
            send_sem=ws_sem.at[n],
            recv_sem=wr_sem.at[n],
            device_id=sibling,
            device_id_type=MESH,
        )

    hand_on(0, 0).start()
    for d in range(4):
        for dx in range(NX):
            if (d, dx) != (0, 0):
                dispatch(d, dx).start()
    swaps = [weight_swap(n, ref) for n, ref in enumerate((wg_ref, wu_ref, wd_ref))]
    for copy in swaps:
        copy.start()
    for copy in own:
        copy.wait()
    for copy in swaps:
        copy.wait()

    def giveback(g, dx):
        direct = g < 4
        d = jnp.where(direct, g, g - 4)
        pz = jnp.where(direct, z - way * d, mate_z + way * d)
        return pltpu.make_async_remote_copy(
            src_ref=ret.at[g * 4 + dx],
            dst_ref=got.at[g * 4 + dx],
            send_sem=ret_sem.at[g * 4 + dx],
            recv_sem=got_sem.at[g * 4 + dx],
            device_id=place(x - dx, pz, core),
            device_id_type=MESH,
        )

    def group(g, carry):
        for dx in range(NX):

            def arrived(dx=dx):
                pltpu.make_async_copy(
                    recv.at[g, dx], recv.at[g, dx], recv_sem.at[g * 4 + dx]
                ).wait()

            if dx == 0:
                pl.when(g > 0)(arrived)
            else:
                arrived()

            @pl.when((g < 4) if dx else ((g > 0) & (g < 4)))
            def _(dx=dx):
                hand_on(g, dx).start()

        block = recv[g].reshape(4 * 16, D)
        gate = nt(block, w[0:2].reshape(2 * HID, D)).reshape(4, 16, 2 * HID)[:, :8]
        upper = nt(block, w[2:4].reshape(2 * HID, D)).reshape(4, 16, 2 * HID)[:, :8]
        down = nt(block, w[4:6].reshape(2 * HID, D)).reshape(4, 16, 2 * HID)[:, 8:]
        sigma = jax.nn.sigmoid(gate)
        active = gate * sigma
        hidden = (active * upper).astype(BF16).astype(F32)
        comb = jnp.sum(hidden * down, axis=-1, keepdims=True)
        gate_part = down * upper * sigma * (1.0 + gate * (1.0 - sigma))
        gate_part = gate_part.reshape(4 * 8, 2 * HID).astype(BF16)
        up_part = (down * active).reshape(4 * 8, 2 * HID).astype(BF16)
        halves = []
        for c in range(2):
            cols = slice(c * HALF, (c + 1) * HALF)
            part = nn(gate_part, w[0:2, :, cols].reshape(2 * HID, HALF))
            part += nn(up_part, w[2:4, :, cols].reshape(2 * HID, HALF))
            halves.append(part.reshape(4, 8, HALF))
        out = jnp.concatenate(halves, axis=1).astype(BF16)
        comb = jnp.broadcast_to(comb, (4, 8, 128))
        comb = jnp.concatenate([comb, jnp.zeros((4, 8, 128), F32)], axis=1).astype(BF16)
        for dx in range(NX):
            ret[g * 4 + dx, :, 0:HALF] = out[dx]
            ret[g * 4 + dx, :, HALF:BACK] = comb[dx]
        for dx in range(NX):
            if dx == 0:

                @pl.when(g == 0)
                def _():
                    got[0] = ret[0]

                @pl.when(g > 0)
                def _():
                    giveback(g, 0).start()
            else:
                giveback(g, dx).start()
        return carry

    lax.fori_loop(0, 8, group, 0)

    lane, expert, chosen, scaled = picks(256, 16)
    first = lax.rem(lane, 16) < 8
    low = jnp.where(first, scaled, 0.0).astype(BF16)
    high = jnp.where(first, 0.0, scaled).astype(BF16)
    chosen = jnp.where(first, chosen, 0.0)

    for n in range(1, 32):
        pltpu.make_async_copy(got.at[n], got.at[n], got_sem.at[n]).wait()

    back = [got[h * 16 : (h + 1) * 16, :, 0:HALF].reshape(256, HALF) for h in range(2)]
    total = [nn(side, back[0]) + nn(side, back[1]) for side in (low, high)]

    mean = jnp.zeros((TOK, 1), F32)
    for c in range(2):
        cols = slice(c * HALF, (c + 1) * HALF)
        hat = x_ref[:, cols].astype(F32) * rinv
        product = total[c] * hat
        sum_xc[x * 2 + core, :, cols] = jnp.sum(product, axis=0, keepdims=True)
        mean += jnp.sum(product * g_ref[:, cols], axis=-1, keepdims=True)
    mean = mean / D

    def share_xc(dx, dc):
        return pltpu.make_async_remote_copy(
            src_ref=sum_xc.at[x * 2 + core],
            dst_ref=sum_xc.at[x * 2 + core],
            send_sem=xs_sem.at[dx * 2 + dc],
            recv_sem=xr_sem.at[dx * 2 + dc],
            device_id=place(x + dx, z, lax.rem(core + dc, 2)),
            device_id_type=MESH,
        )

    others = [(dx, dc) for dx in range(NX) for dc in range(2) if (dx, dc) != (0, 0)]
    for dx, dc in others:
        share_xc(dx, dc).start()

    for c in range(2):
        cols = slice(c * HALF, (c + 1) * HALF)
        hat = x_ref[:, cols].astype(F32) * rinv
        grad = dy_ref[:, cols].astype(F32) + rinv * (total[c] * g_ref[:, cols] - hat * mean)
        grads[:, cols] = grad.astype(BF16)

    def pass_on():
        return pltpu.make_async_remote_copy(
            src_ref=grads,
            dst_ref=passed_ref,
            send_sem=pass_sem.at[0],
            recv_sem=pass_sem.at[1],
            device_id=ahead,
            device_id_type=MESH,
        )

    @pl.when(sec > 0)
    def _():
        pass_on().start()

    comb_back = [got[h * 16 : (h + 1) * 16, :, HALF:BACK].reshape(256, 128) for h in range(2)]
    column = lax.broadcasted_iota(jnp.int32, (TOK, 128), 1)
    comb = jnp.zeros((TOK, 128), F32)
    for k in range(TOP):
        one = jnp.where(ids[:, k : k + 1] == expert, chosen, 0.0).astype(BF16)
        comb = jnp.where(column == k, nn(one, comb_back[0]) + nn(one, comb_back[1]), comb)
    comb_ref[...] = comb[:, 0:TOP].astype(BF16)

    for dx, dc in others:
        share_xc(dx, dc).wait()
    sum_z[z] = jnp.sum(sum_xc[...], axis=0)

    def share_z(dz):
        return pltpu.make_async_remote_copy(
            src_ref=sum_z.at[z],
            dst_ref=sum_z.at[z],
            send_sem=zs_sem.at[dz],
            recv_sem=zr_sem.at[dz],
            device_id=place(x, z + dz, core),
            device_id_type=MESH,
        )

    for dz in range(1, NZ):
        share_z(dz).start()

    for d in range(4):
        for dx in range(NX):
            if (d, dx) != (0, 0):
                dispatch(d, dx).wait_send()
            hand_on(d, dx).wait_send()

    def sent(n, carry):
        pltpu.make_async_copy(ret.at[n], ret.at[n], ret_sem.at[n]).wait()
        return carry

    lax.fori_loop(1, 32, sent, 0)
    for dz in range(1, NZ):
        share_z(dz).wait()
    gain_ref[...] = jnp.sum(sum_z[...], axis=0)

    @pl.when(sec > 0)
    def _():
        pass_on().wait_send()

    @pl.when(sec < 7)
    def _():
        pass_on().wait_recv()

    @pl.when(sec == 7)
    def _():
        grads[...] = jnp.zeros_like(grads)
        clear = pltpu.make_async_copy(grads, passed_ref, pass_sem.at[1])
        clear.start()
        clear.wait()


def per_device(layer_input, out_grad, norm_gain, expert_ids, combine, w_gate, w_up, w_down):
    vmem = pl.BlockSpec(memory_space=pltpu.VMEM)
    hbm = pl.BlockSpec(memory_space=pl.ANY)
    dma = pltpu.SemaphoreType.DMA
    passed, comb, gain = pl.pallas_call(
        kernel,
        out_shape=(
            jax.ShapeDtypeStruct((TOK, D), BF16),
            jax.ShapeDtypeStruct((TOK, TOP), BF16),
            jax.ShapeDtypeStruct((1, D), F32),
        ),
        in_specs=[vmem] * 5 + [hbm] * 3,
        out_specs=(hbm, vmem, vmem),
        scratch_shapes=[
            pltpu.VMEM((16, 16, D), BF16),
            pltpu.VMEM((8, NX, 16, D), BF16),
            pltpu.VMEM((6, HID, D), BF16),
            pltpu.VMEM((32, 16, BACK), BF16),
            pltpu.VMEM((32, 16, BACK), BF16),
            pltpu.VMEM((TOK, D), BF16),
            pltpu.VMEM((8, 1, D), F32),
            pltpu.VMEM((8, 1, D), F32),
            dma((16,)), dma((32,)), dma((16,)), dma((32,)), dma((32,)),
            dma((3,)), dma((3,)), dma((3,)),
            dma((8,)), dma((8,)), dma((8,)), dma((8,)), dma((2,)),
        ],
        compiler_params=pltpu.CompilerParams(
            collective_id=0, has_side_effects=True, vmem_limit_bytes=48 * 1024 * 1024
        ),
    )(
        layer_input[0], out_grad[0], norm_gain, expert_ids[0], combine[0],
        w_gate[0], w_up[0], w_down[0],
    )
    return passed[None], comb[None], gain


def solution(mesh):
    rows = P("section", "expert", None)
    whole = P("section", None)
    return jax.shard_map(
        per_device,
        mesh=mesh,
        in_specs=(rows, rows, whole, rows, rows, rows, rows, rows),
        out_specs=(rows, rows, whole),
        check_vma=False,
    )
```

time: 357 us -> 96.8 us (0.27)
  blocking collectives: 199 us -> 0 us
  waiting for transfers between devices: 104 us -> 0 us
  Pallas kernels: 0 us -> 86.1 us
  starting transfers between devices: 27.6 us -> 0 us
  matrix products: 12.4 us -> 0 us
  other arithmetic: 3.98 us -> 0 us
    psum x1 -> x0, blocking collectives: 127 us -> none  [per_device(): gain_total = lax.psum(gain_correction, 'expert')]
    all_to_all x3 -> x0, waiting for transfers between devices: 104 us -> none  [the longest x1 49.9 us: per_device(): lax.all_to_all(send_x, 'expert', split_axis=0, concat_axis=0, tiled=True)]
    pallas_call x0 -> x1, Pallas kernels: none -> 86.1 us  [per_device(): pl.pallas_call(kernel, out_shape=(jax.ShapeDtypeStruct((TOK, D), BF16), j...]
    all_to_all x2 -> x0, blocking collectives: 72 us -> none  [the longest x1 56.9 us: per_device(): lax.all_to_all(rows_grad.reshape(peers, CAP, width), 'expert', split_axis...]
    all_to_all x3 -> x0, starting transfers between devices: 24.4 us -> none  [the longest x1 13.8 us: per_device(): lax.all_to_all(send_w, 'expert', split_axis=0, concat_axis=0, tiled=True)]
    dot_general x11 -> x0, matrix products: 12.4 us -> none  [the longest x3 6.3 us: contract_cols(): lax.dot_general(left, right, (((1,), (1,)), ((), ())), preferred_element_...]
    unnamed x24 -> x21, local copies, waits for them, and re-layouts: 4.06 us -> 9.31 us
  transfers between devices with their start and end apart: 4 -> 0, of which waited for: 3 -> 0; matrix products, arithmetic and copies ran while one was open for 3% -> 0% of each run, Pallas kernels for 0% -> 0%
where the time goes in v1:
time: 96.8 us; the launch traced here: 96 us
  Pallas kernels  86.1 us (89%)
  local copies, waits for them, and re-layouts  9.31 us (10%)
    pallas_call x1, Pallas kernels, per_device(): pl.pallas_call(kernel, out_shape=(jax.ShapeDtypeStruct((TOK, D), BF16), j...  86.1 us
    unnamed x21, local copies, waits for them, and re-layouts  9.31 us

profile of v1, /device:TPU:56, one launch (start us, length us, event | category | flops | bytes accessed | tf_op | source)
XLA Modules:
  0.0 96.0 jit_solution(8481655220626007129)
XLA Ops:
  0.6 0.0 copy-start.7
  0.6 0.7 copy-done.7
  1.3 0.0 copy-start.6
  1.3 0.1 copy.12
  1.4 0.6 copy-done.6
  2.0 0.0 copy-start.5
  2.0 0.1 copy.11
  2.1 0.6 copy-done.5
  2.7 0.0 copy-start
  2.7 1.1 %copy-done = bf16[1,192,2048]{2,1,0:T(8,128)(2,1)S(1)} copy-done((bf16[1,192,2048]{2,1,0:T(8,128)(2,1)S(1)}, bf16[1,192,2048]{2,1,0:T(8,128)(2,1)}, u32[]{:S(2)}) %copy-start) | copy-done | bytes 786456
  3.8 0.0 copy-start.1
  3.8 1.1 %copy-done.1 = bf16[1,192,2048]{2,1,0:T(8,128)(2,1)S(1)} copy-done((bf16[1,192,2048]{2,1,0:T(8,128)(2,1)S(1)}, bf16[1,192,2048]{2,1,0:T(8,128)(2,1)}, u32[]{:S(2)}) %copy-start.1) | copy-done | bytes 786456
  5.0 0.0 copy-start.2
  5.0 1.1 %copy-done.2 = bf16[1,192,2048]{2,1,0:T(8,128)(2,1)S(1)} copy-done((bf16[1,192,2048]{2,1,0:T(8,128)(2,1)S(1)}, bf16[1,192,2048]{2,1,0:T(8,128)(2,1)}, u32[]{:S(2)}) %copy-start.2) | copy-done | bytes 786456
  6.1 0.0 copy-start.3
  6.1 0.9 copy-done.3
  7.0 0.0 copy-start.4
  7.1 0.9 copy-done.4
  8.0 86.1 %shard_map.103 = (bf16[64,2048]{1,0:T(8,128)(2,1)S(1)}, bf16[64,8]{1,0:T(8,128)(2,1)S(1)}, f32[1,2048]{1,0:T(1,128)S(1)}) custom-call(bf16[64,2048]{1,0:T(8,128)(2,1)S(1)} %bitcast.12, bf16[64,2048]{1,0:T(8,128)(2,1)S(1)} %bitcast.13, f32[1,2048]{1,0:T(1,128)S(1)} %copy-done.5, s32[64,8]{1,0:T(8,128)S(1)} %bitcast.15, bf16[64,8]{1,0:T(8,128)(2,1)S(1)} %bitcast.16, ...), custom_call_target="tpu_custom_call" | custom-call | tf_op jit(solution)/shard_map/pallas_call | solution.py:349
  94.1 0.7 copy.13
  94.7 0.7 copy.16
  95.4 0.6 copy.17
Async XLA Ops:
  0.6 0.7 copy-start.7
  1.3 0.7 copy-start.6
  2.0 0.7 copy-start.5
  2.7 1.1 %copy-start = (bf16[1,192,2048]{2,1,0:T(8,128)(2,1)S(1)}, bf16[1,192,2048]{2,1,0:T(8,128)(2,1)}, u32[]{:S(2)}) copy-start(bf16[1,192,2048]{2,1,0:T(8,128)(2,1)} %param.13) | copy-start | bytes 2359300
  3.8 1.1 %copy-start.1 = (bf16[1,192,2048]{2,1,0:T(8,128)(2,1)S(1)}, bf16[1,192,2048]{2,1,0:T(8,128)(2,1)}, u32[]{:S(2)}) copy-start(bf16[1,192,2048]{2,1,0:T(8,128)(2,1)} %param.14) | copy-start | bytes 2359300
  5.0 1.1 %copy-start.2 = (bf16[1,192,2048]{2,1,0:T(8,128)(2,1)S(1)}, bf16[1,192,2048]{2,1,0:T(8,128)(2,1)}, u32[]{:S(2)}) copy-start(bf16[1,192,2048]{2,1,0:T(8,128)(2,1)} %param.15) | copy-start | bytes 2359300
  6.1 0.9 copy-start.3
  7.0 0.9 copy-start.4

commit v2 on v1

v2 whole, which is shorter than its diff:
```python
import jax
import jax.numpy as jnp
from jax import lax
from jax.experimental import pallas as pl
from jax.experimental.pallas import tpu as pltpu
from jax.sharding import PartitionSpec as P

MESH = pl.DeviceIdType.MESH
NX, NZ = 4, 8
CAP = 8
D = 2048
HALF = D // 2
HID = 192
TOK = 64
TOP = 8
BACK = HALF + 128
EPS = 1e-06
F32, BF16 = jnp.float32, jnp.bfloat16


def nt(left, right):
    return lax.dot_general(left, right, (((1,), (1,)), ((), ())), preferred_element_type=F32)


def nn(left, right):
    return jnp.dot(left, right, preferred_element_type=F32)


def kernel(
    x_hbm, dy_hbm, g_hbm, ids_hbm, cw_hbm, wg_ref, wu_ref, wd_ref,
    passed_ref, comb_ref, gain_ref,
    x_ref, dy_ref, g_ref, ids_ref, cw_ref,
    send, recv, w, ret, got, hold, part, grads, gain_sum, sum_xc, sum_z,
    in_sem, disp_sem, recv_sem, fwd_sem, ret_sem, got_sem, part_sem, wl_sem, ws_sem, wr_sem,
    xs_sem, xr_sem, zs_sem, zr_sem, pass_sem,
):
    sec = lax.axis_index("section")
    me = lax.axis_index("expert")
    core = lax.rem(me, 2)
    z = lax.rem(me // 2, NZ)
    x = me // (2 * NZ)
    way = 1 - 2 * lax.rem(z, 2)
    mate_z = z + way

    def place(px, pz, pc):
        return (sec, (lax.rem(px + NX, NX) * NZ + lax.rem(pz + 2 * NZ, NZ)) * 2 + pc)

    def entry_z(d):
        return z + way * d if d % 2 == 0 else z - way * d

    sibling = place(x, z, 1 - core)
    mate = place(x, mate_z, core)
    ahead = (lax.rem(sec + 7, 8), me)
    behind = (lax.rem(sec + 1, 8), me)

    fetch = []
    pairs = ((x_hbm, x_ref), (g_hbm, g_ref), (ids_hbm, ids_ref), (cw_hbm, cw_ref), (dy_hbm, dy_ref))
    for n, (src, dst) in enumerate(pairs):
        copy = pltpu.make_async_copy(src, dst, in_sem.at[n])
        copy.start()
        fetch.append(copy)

    barrier = pltpu.get_barrier_semaphore()

    def greet(q, carry):
        chip = lax.rem(x * NZ + z + q, NX * NZ)
        pl.semaphore_signal(barrier, inc=1, device_id=(sec, chip * 2 + core), device_id_type=MESH)
        return carry

    lax.fori_loop(1, NX * NZ, greet, 0)
    for q in range(NX):
        pl.semaphore_signal(
            barrier, inc=1, device_id=place(x + q, z, 1 - core), device_id_type=MESH
        )
    for other in (ahead, behind):
        pl.semaphore_signal(barrier, inc=1, device_id=other, device_id_type=MESH)

    own = []
    for n, ref in enumerate((wg_ref, wu_ref, wd_ref)):
        copy = pltpu.make_async_copy(ref, w.at[2 * n], wl_sem.at[n])
        copy.start()
        own.append(copy)

    for copy in fetch:
        copy.wait()

    rows = x_ref[...].astype(F32)
    rinv = lax.rsqrt(jnp.mean(rows * rows, axis=-1, keepdims=True) + EPS)
    normed = (rows * rinv * g_ref[...]).astype(BF16)
    dy = dy_ref[...]
    ids = ids_ref[...]
    weights = cw_ref[...].astype(F32)

    def expert_of(block):
        d, dx = block // 4, lax.rem(block, 4)
        ez = jnp.where(lax.rem(d, 2) == 0, z + way * d, z - way * d)
        ez = lax.rem(ez + 2 * NZ, NZ)
        return lax.rem(x + dx, NX) * 4 + ez // 2

    before = (
        lax.broadcasted_iota(jnp.int32, (TOK, TOK), 0)
        < lax.broadcasted_iota(jnp.int32, (TOK, TOK), 1)
    ).astype(BF16)

    def picks(slots, per):
        slot = lax.broadcasted_iota(jnp.int32, (slots, TOK), 0)
        expert = expert_of(slot // per)
        named = jnp.zeros((slots, TOK), F32)
        scaled = jnp.zeros((slots, TOK), F32)
        for k in range(TOP):
            hit = ids[k : k + 1, :] == expert
            named = jnp.where(hit, 1.0, named)
            scaled = jnp.where(hit, weights[k : k + 1, :], scaled)
        rank = nn(named.astype(BF16), before)
        mine = rank == lax.rem(slot, CAP).astype(F32)
        return slot, expert, jnp.where(mine, named, 0.0), jnp.where(mine, scaled, 0.0)

    _, _, token_pick, scaled_pick = picks(128, CAP)
    token_pick, scaled_pick = token_pick.astype(BF16), scaled_pick.astype(BF16)

    def tn(left, right):
        return lax.dot_general(left, right, (((0,), (0,)), ((), ())), preferred_element_type=F32)

    for c in range(4):
        cols = slice(c * 512, (c + 1) * 512)
        part_x = nn(token_pick, normed[:, cols]).reshape(16, CAP, 512)
        part_dy = nn(scaled_pick, dy[:, cols]).reshape(16, CAP, 512)
        send[:, :, cols] = jnp.concatenate([part_x, part_dy], axis=1).astype(BF16)
    recv[0, 0] = send[0]

    pl.semaphore_wait(barrier, NX * NZ - 1 + NX + 2)

    def dispatch(d, dx):
        return pltpu.make_async_remote_copy(
            src_ref=send.at[d * 4 + dx],
            dst_ref=recv.at[d, dx],
            send_sem=disp_sem.at[d * 4 + dx],
            recv_sem=recv_sem.at[d * 4 + dx],
            device_id=place(x + dx, entry_z(d), core),
            device_id_type=MESH,
        )

    def hand_on(d, dx):
        return pltpu.make_async_remote_copy(
            src_ref=recv.at[d, dx],
            dst_ref=recv.at[d + 4, dx],
            send_sem=fwd_sem.at[d * 4 + dx],
            recv_sem=recv_sem.at[16 + d * 4 + dx],
            device_id=mate,
            device_id_type=MESH,
        )

    def weight_swap(n, ref):
        return pltpu.make_async_remote_copy(
            src_ref=ref,
            dst_ref=w.at[2 * n + 1],
            send_sem=ws_sem.at[n],
            recv_sem=wr_sem.at[n],
            device_id=sibling,
            device_id_type=MESH,
        )

    hand_on(0, 0).start()
    swaps = [weight_swap(n, ref) for n, ref in enumerate((wg_ref, wu_ref, wd_ref))]
    for d in range(4):
        for dx in range(NX):
            if (d, dx) != (0, 0):
                dispatch(d, dx).start()
    for copy in swaps:
        copy.start()

    def landed(buffer, semaphore):
        pltpu.make_async_copy(buffer, buffer, semaphore).wait()

    def forward(d):
        for dx in range(NX):
            if (d, dx) != (0, 0):
                landed(recv.at[d, dx], recv_sem.at[d * 4 + dx])
                hand_on(d, dx).start()

    def giveback(g, dx):
        direct = g < 4
        d = jnp.where(direct, g, g - 4)
        pz = jnp.where(direct, z - way * d, mate_z + way * d)
        return pltpu.make_async_remote_copy(
            src_ref=ret.at[g * 4 + dx],
            dst_ref=got.at[g * 4 + dx],
            send_sem=ret_sem.at[g * 4 + dx],
            recv_sem=got_sem.at[g * 4 + dx],
            device_id=place(x - dx, pz, core),
            device_id_type=MESH,
        )

    def halfway(g, dx):
        return pltpu.make_async_remote_copy(
            src_ref=ret.at[g * 4 + dx],
            dst_ref=part.at[(g - 6) * 4 + dx],
            send_sem=ret_sem.at[g * 4 + dx],
            recv_sem=part_sem.at[(g - 6) * 4 + dx],
            device_id=mate,
            device_id_type=MESH,
        )

    def join(d):
        for dx in range(NX):
            n = (d - 2) * 4 + dx
            landed(part.at[n], part_sem.at[n])
            ret[d * 4 + dx] = (hold[n] + part[n].astype(F32)).astype(BF16)
            giveback(d, dx).start()

    forward(0)
    forward(1)
    for copy in own:
        copy.wait()
    for copy in swaps:
        copy.wait()

    gain_sum[...] = jnp.zeros_like(gain_sum)
    order = (0, 1, 4, 2, 5, 3, 6, 7)

    def group(i, carry):
        g = jnp.int32(order[0])
        for n in range(1, 8):
            g = jnp.where(i == n, order[n], g)

        @pl.when(i == 1)
        def _():
            forward(2)

        @pl.when(i == 2)
        def _():
            forward(3)

        @pl.when(g >= 4)
        def _():
            for dx in range(NX):
                landed(recv.at[g, dx], recv_sem.at[g * 4 + dx])

        block = recv[g].reshape(4 * 16, D)
        gate = nt(block, w[0:2].reshape(2 * HID, D)).reshape(4, 16, 2 * HID)[:, :8]
        upper = nt(block, w[2:4].reshape(2 * HID, D)).reshape(4, 16, 2 * HID)[:, :8]
        down = nt(block, w[4:6].reshape(2 * HID, D)).reshape(4, 16, 2 * HID)[:, 8:]
        sigma = jax.nn.sigmoid(gate)
        active = gate * sigma
        hidden = (active * upper).astype(BF16).astype(F32)
        comb = jnp.sum(hidden * down, axis=-1, keepdims=True)
        gate_part = down * upper * sigma * (1.0 + gate * (1.0 - sigma))
        gate_part = gate_part.reshape(4 * 8, 2 * HID).astype(BF16)
        up_part = (down * active).reshape(4 * 8, 2 * HID).astype(BF16)
        halves = []
        for c in range(2):
            cols = slice(c * HALF, (c + 1) * HALF)
            piece = nn(gate_part, w[0:2, :, cols].reshape(2 * HID, HALF))
            piece += nn(up_part, w[2:4, :, cols].reshape(2 * HID, HALF))
            piece = piece.reshape(4, 8, HALF)
            halves.append(piece)
            held = recv[g, :, :, cols].astype(F32)[:, :8]
            gain_sum[:, cols] += jnp.sum(piece * held, axis=0)
        out = jnp.concatenate(halves, axis=1)
        comb = jnp.broadcast_to(comb, (4, 8, 128))
        comb = jnp.concatenate([comb, jnp.zeros((4, 8, 128), F32)], axis=1)
        kept = (g == 2) | (g == 3)
        half = (g == 6) | (g == 7)

        @pl.when(kept)
        def _():
            for dx in range(NX):
                hold[(g - 2) * 4 + dx, :, 0:HALF] = out[dx]
                hold[(g - 2) * 4 + dx, :, HALF:BACK] = comb[dx]

        @pl.when(jnp.logical_not(kept))
        def _():
            for dx in range(NX):
                ret[g * 4 + dx, :, 0:HALF] = out[dx].astype(BF16)
                ret[g * 4 + dx, :, HALF:BACK] = comb[dx].astype(BF16)

        @pl.when(half)
        def _():
            for dx in range(NX):
                halfway(g, dx).start()

        @pl.when(jnp.logical_not(kept | half))
        def _():
            for dx in range(NX):
                if dx == 0:

                    @pl.when(g == 0)
                    def _():
                        got[0] = ret[0]

                    @pl.when(g > 0)
                    def _():
                        giveback(g, 0).start()
                else:
                    giveback(g, dx).start()

        return carry

    lax.fori_loop(0, 8, group, 0)

    sum_xc[x * 2 + core] = jnp.sum(gain_sum[...], axis=0, keepdims=True)

    def share_xc(dx, dc):
        return pltpu.make_async_remote_copy(
            src_ref=sum_xc.at[x * 2 + core],
            dst_ref=sum_xc.at[x * 2 + core],
            send_sem=xs_sem.at[dx * 2 + dc],
            recv_sem=xr_sem.at[dx * 2 + dc],
            device_id=place(x + dx, z, lax.rem(core + dc, 2)),
            device_id_type=MESH,
        )

    others = [(dx, dc) for dx in range(NX) for dc in range(2) if (dx, dc) != (0, 0)]
    for dx, dc in others:
        share_xc(dx, dc).start()

    join(2)
    join(3)

    for dx, dc in others:
        share_xc(dx, dc).wait()
    sum_z[z] = jnp.sum(sum_xc[...], axis=0)

    def share_z(dz):
        return pltpu.make_async_remote_copy(
            src_ref=sum_z.at[z],
            dst_ref=sum_z.at[z],
            send_sem=zs_sem.at[dz],
            recv_sem=zr_sem.at[dz],
            device_id=place(x, z + dz, core),
            device_id_type=MESH,
        )

    for dz in range(1, NZ):
        share_z(dz).start()

    slot, expert, chosen, _ = picks(256, 16)
    first = lax.rem(slot, 16) < 8
    low = jnp.where(first, chosen, 0.0).astype(BF16)
    high = jnp.where(first, 0.0, chosen).astype(BF16)
    chosen = jnp.where(first, chosen, 0.0)

    for n in [1, 2, 3, 4, 5, 6, 7, 8, 9, 10, 11, 12, 13, 14, 15, 16, 17, 18, 19, 20, 21, 22, 23]:
        landed(got.at[n], got_sem.at[n])

    spans = [(0, 16, 0), (16, 24, 0)]
    total = []
    for side in (low, high):
        sums = 0.0
        for lo, hi, at in spans:
            size = (hi - lo) * 16
            sums += tn(side[at : at + size], got[lo:hi, :, 0:HALF].reshape(size, HALF))
        total.append(sums)

    hats = [x_ref[:, c * HALF : (c + 1) * HALF].astype(F32) * rinv for c in range(2)]
    products = [total[c] * hats[c] for c in range(2)]
    mean = 0.0
    for c in range(2):
        cols = slice(c * HALF, (c + 1) * HALF)
        mean += jnp.sum(products[c] * g_ref[:, cols], axis=-1, keepdims=True)
    mean = mean / D
    for c in range(2):
        cols = slice(c * HALF, (c + 1) * HALF)
        scaled_grad = total[c] * g_ref[:, cols]
        grad = dy_ref[:, cols].astype(F32) + rinv * (scaled_grad - hats[c] * mean)
        grads[:, cols] = grad.astype(BF16)

    def pass_on():
        return pltpu.make_async_remote_copy(
            src_ref=grads,
            dst_ref=passed_ref,
            send_sem=pass_sem.at[0],
            recv_sem=pass_sem.at[1],
            device_id=ahead,
            device_id_type=MESH,
        )

    @pl.when(sec > 0)
    def _():
        pass_on().start()

    line = lax.broadcasted_iota(jnp.int32, (TOP, TOK), 0)
    comb = jnp.zeros((TOP, TOK), F32)
    found = got[0:16, :, HALF:BACK].astype(F32).reshape(256, 128)[:, 0:TOK]
    extra = got[16:24, :, HALF:BACK].astype(F32).reshape(128, 128)[:, 0:TOK]
    found = chosen * jnp.concatenate([found[0:128] + extra, found[128:256]], axis=0)
    for k in range(TOP):
        one = jnp.where(ids[k : k + 1, :] == expert, found, 0.0)
        comb = jnp.where(line == k, jnp.sum(one, axis=0, keepdims=True), comb)
    comb_ref[...] = (comb / weights).astype(BF16)

    for d in range(4):
        for dx in range(NX):
            if (d, dx) != (0, 0):
                dispatch(d, dx).wait_send()
            hand_on(d, dx).wait_send()

    def sent(n, carry):
        landed(ret.at[n], ret_sem.at[n])
        return carry

    lax.fori_loop(1, 32, sent, 0)
    for dz in range(1, NZ):
        share_z(dz).wait()
    gain_ref[...] = jnp.sum(sum_z[...], axis=0) / g_ref[...]

    @pl.when(sec > 0)
    def _():
        pass_on().wait_send()

    @pl.when(sec < 7)
    def _():
        pass_on().wait_recv()

    @pl.when(sec == 7)
    def _():
        grads[...] = jnp.zeros_like(grads)
        clear = pltpu.make_async_copy(grads, passed_ref, pass_sem.at[1])
        clear.start()
        clear.wait()


def per_device(layer_input, out_grad, norm_gain, expert_ids, combine, w_gate, w_up, w_down):
    vmem = pl.BlockSpec(memory_space=pltpu.VMEM)
    hbm = pl.BlockSpec(memory_space=pl.ANY)
    dma = pltpu.SemaphoreType.DMA
    passed, comb, gain = pl.pallas_call(
        kernel,
        out_shape=(
            jax.ShapeDtypeStruct((TOK, D), BF16),
            jax.ShapeDtypeStruct((TOP, TOK), BF16),
            jax.ShapeDtypeStruct((1, D), F32),
        ),
        in_specs=[hbm] * 8,
        out_specs=(hbm, vmem, vmem),
        scratch_shapes=[
            pltpu.VMEM((TOK, D), BF16),
            pltpu.VMEM((TOK, D), BF16),
            pltpu.VMEM((1, D), F32),
            pltpu.VMEM((TOP, TOK), jnp.int32),
            pltpu.VMEM((TOP, TOK), BF16),
            pltpu.VMEM((16, 16, D), BF16),
            pltpu.VMEM((8, NX, 16, D), BF16),
            pltpu.VMEM((6, HID, D), BF16),
            pltpu.VMEM((32, 16, BACK), BF16),
            pltpu.VMEM((32, 16, BACK), BF16),
            pltpu.VMEM((8, 16, BACK), F32),
            pltpu.VMEM((8, 16, BACK), BF16),
            pltpu.VMEM((TOK, D), BF16),
            pltpu.VMEM((8, D), F32),
            pltpu.VMEM((8, 1, D), F32),
            pltpu.VMEM((8, 1, D), F32),
            dma((5,)), dma((16,)), dma((32,)), dma((16,)), dma((32,)), dma((32,)), dma((8,)),
            dma((3,)), dma((3,)), dma((3,)),
            dma((8,)), dma((8,)), dma((8,)), dma((8,)), dma((2,)),
        ],
        compiler_params=pltpu.CompilerParams(
            collective_id=0, has_side_effects=True, vmem_limit_bytes=60 * 1024 * 1024
        ),
    )(
        layer_input[0], out_grad[0], norm_gain, expert_ids[0].T, combine[0].T,
        w_gate[0], w_up[0], w_down[0],
    )
    return passed[None], comb.T[None], gain


def solution(mesh):
    rows = P("section", "expert", None)
    whole = P("section", None)
    return jax.shard_map(
        per_device,
        mesh=mesh,
        in_specs=(rows, rows, whole, rows, rows, rows, rows, rows),
        out_specs=(rows, rows, whole),
        check_vma=False,
    )
```

time: 96.8 us -> 84.3 us (0.87)
  the two profiles are of different devices: /device:TPU:56 before, /device:TPU:152 now
where the time goes in v2:
time: 84.3 us; the launch traced here: 84.1 us
  Pallas kernels  80.6 us (96%)
  local copies, waits for them, and re-layouts  2.86 us (3%)
    pallas_call x1, Pallas kernels, per_device(): pl.pallas_call(kernel, out_shape=(jax.ShapeDtypeStruct((TOK, D), BF16), j...  80.6 us
    unnamed x7, local copies, waits for them, and re-layouts  2.86 us

profile of v2, /device:TPU:152, one launch (start us, length us, event | category | flops | bytes accessed | tf_op | source)
XLA Modules:
  0.0 84.1 jit_solution(13676424482486594910)
XLA Ops:
  0.6 80.6 %shard_map.103 = (bf16[64,2048]{1,0:T(8,128)(2,1)}, bf16[8,64]{1,0:T(8,128)(2,1)}, f32[1,2048]{1,0:T(1,128)}) custom-call(bf16[64,2048]{1,0:T(8,128)(2,1)} %bitcast.18, bf16[64,2048]{1,0:T(8,128)(2,1)} %bitcast.19, f32[1,2048]{1,0:T(1,128)} %g_hbm.1, s32[8,64]{1,0:T(8,128)} %bitcast.21, bf16[8,64]{1,0:T(8,128)(2,1)} %bitcast.22, bf16[192,2048]{1,0:T(8,128)(2,1)} %bitcast.15, ...), custom_call_target="tpu_custom_call" | custom-call | tf_op jit(solution)/shard_map/pallas_call | solution.py:427
  81.3 0.0 copy-start.1
  81.3 0.0 copy-start
  81.3 1.7 %copy.14 = bf16[1,64,2048]{2,1,0:T(8,128)(2,1)} copy(bf16[1,64,2048]{2,1,0:T(8,128)(2,1)} %bitcast.20) | data formatting | bytes 524288
  82.9 0.0 copy-done.1
  83.0 0.6 copy.15
  83.5 0.0 copy-done
  83.5 0.6 copy.16
Async XLA Ops:
  81.3 1.7 %copy-start.1 = (bf16[8,64]{1,0:T(8,128)(2,1)S(1)}, bf16[8,64]{1,0:T(8,128)(2,1)}, u32[]{:S(2)}) copy-start(bf16[8,64]{1,0:T(8,128)(2,1)} %get-tuple-element.7) | copy-start | bytes 3076
  81.3 2.3 %copy-start = (f32[1,2048]{1,0:T(1,128)S(1)}, f32[1,2048]{1,0:T(1,128)}, u32[]{:S(2)}) copy-start(f32[1,2048]{1,0:T(1,128)} %get-tuple-element.14) | copy-start | bytes 24580

commit v3 on v2

--- a/solution.py
+++ b/solution.py
@@ -13,7 +13,6 @@
 HID = 192
 TOK = 64
 TOP = 8
-BACK = HALF + 128
 EPS = 1e-06
 F32, BF16 = jnp.float32, jnp.bfloat16
 
@@ -30,9 +29,10 @@
     x_hbm, dy_hbm, g_hbm, ids_hbm, cw_hbm, wg_ref, wu_ref, wd_ref,
     passed_ref, comb_ref, gain_ref,
     x_ref, dy_ref, g_ref, ids_ref, cw_ref,
-    send, recv, w, ret, got, hold, part, grads, gain_sum, sum_xc, sum_z,
+    next_x, next_dy, next_g, next_ids,
+    send, recv, w, ret, got, hold, part, comb_out, comb_in, gain_sum, sum_xc, sum_z,
     in_sem, disp_sem, recv_sem, fwd_sem, ret_sem, got_sem, part_sem, wl_sem, ws_sem, wr_sem,
-    xs_sem, xr_sem, zs_sem, zr_sem, pass_sem,
+    push_sem, pushed_sem, cs_sem, cr_sem, xs_sem, xr_sem, zs_sem, zr_sem,
 ):
     sec = lax.axis_index("section")
     me = lax.axis_index("expert")
@@ -50,8 +50,8 @@
 
     sibling = place(x, z, 1 - core)
     mate = place(x, mate_z, core)
-    ahead = (lax.rem(sec + 7, 8), me)
-    behind = (lax.rem(sec + 1, 8), me)
+    ahead = lax.rem(sec + 7, 8)
+    behind = lax.rem(sec + 1, 8)
 
     fetch = []
     pairs = ((x_hbm, x_ref), (g_hbm, g_ref), (ids_hbm, ids_ref), (cw_hbm, cw_ref), (dy_hbm, dy_ref))
@@ -72,8 +72,14 @@
         pl.semaphore_signal(
             barrier, inc=1, device_id=place(x + q, z, 1 - core), device_id_type=MESH
         )
-    for other in (ahead, behind):
-        pl.semaphore_signal(barrier, inc=1, device_id=other, device_id_type=MESH)
+
+    def greet_behind(chip, carry):
+        pl.semaphore_signal(
+            barrier, inc=1, device_id=(behind, chip * 2 + core), device_id_type=MESH
+        )
+        return carry
+
+    lax.fori_loop(0, NX * NZ, greet_behind, 0)
 
     own = []
     for n, ref in enumerate((wg_ref, wu_ref, wd_ref)):
@@ -102,7 +108,7 @@
         < lax.broadcasted_iota(jnp.int32, (TOK, TOK), 1)
     ).astype(BF16)
 
-    def picks(slots, per):
+    def picks(ids, weights, slots, per):
         slot = lax.broadcasted_iota(jnp.int32, (slots, TOK), 0)
         expert = expert_of(slot // per)
         named = jnp.zeros((slots, TOK), F32)
@@ -115,8 +121,8 @@
         mine = rank == lax.rem(slot, CAP).astype(F32)
         return slot, expert, jnp.where(mine, named, 0.0), jnp.where(mine, scaled, 0.0)
 
-    _, _, token_pick, scaled_pick = picks(128, CAP)
-    token_pick, scaled_pick = token_pick.astype(BF16), scaled_pick.astype(BF16)
+    slot, expert, chosen, scaled = picks(ids, weights, 128, CAP)
+    token_pick, scaled_pick = chosen.astype(BF16), scaled.astype(BF16)
 
     def tn(left, right):
         return lax.dot_general(left, right, (((0,), (0,)), ((), ())), preferred_element_type=F32)
@@ -128,7 +134,7 @@
         send[:, :, cols] = jnp.concatenate([part_x, part_dy], axis=1).astype(BF16)
     recv[0, 0] = send[0]
 
-    pl.semaphore_wait(barrier, NX * NZ - 1 + NX + 2)
+    pl.semaphore_wait(barrier, 2 * NX * NZ - 1 + NX)
 
     def dispatch(d, dx):
         return pltpu.make_async_remote_copy(
@@ -169,6 +175,25 @@
     for copy in swaps:
         copy.start()
 
+    def push(n, src, dst):
+        return pltpu.make_async_remote_copy(
+            src_ref=src,
+            dst_ref=dst,
+            send_sem=push_sem.at[n],
+            recv_sem=pushed_sem.at[n],
+            device_id=(ahead, me),
+            device_id_type=MESH,
+        )
+
+    pushes = [
+        push(n, src, dst)
+        for n, (src, dst) in enumerate(
+            ((ids_hbm, next_ids), (g_hbm, next_g), (x_hbm, next_x), (dy_hbm, next_dy))
+        )
+    ]
+    for copy in pushes:
+        copy.start()
+
     def landed(buffer, semaphore):
         pltpu.make_async_copy(buffer, buffer, semaphore).wait()
 
@@ -178,16 +203,28 @@
                 landed(recv.at[d, dx], recv_sem.at[d * 4 + dx])
                 hand_on(d, dx).start()
 
-    def giveback(g, dx):
+    def source(g, dx):
         direct = g < 4
         d = jnp.where(direct, g, g - 4)
-        pz = jnp.where(direct, z - way * d, mate_z + way * d)
+        return place(x - dx, jnp.where(direct, z - way * d, mate_z + way * d), core)
+
+    def giveback(g, dx):
         return pltpu.make_async_remote_copy(
             src_ref=ret.at[g * 4 + dx],
             dst_ref=got.at[g * 4 + dx],
             send_sem=ret_sem.at[g * 4 + dx],
             recv_sem=got_sem.at[g * 4 + dx],
-            device_id=place(x - dx, pz, core),
+            device_id=(ahead, source(g, dx)[1]),
+            device_id_type=MESH,
+        )
+
+    def comb_back(g, dx):
+        return pltpu.make_async_remote_copy(
+            src_ref=comb_out.at[g],
+            dst_ref=comb_in.at[g * 4 + dx],
+            send_sem=cs_sem.at[g * 4 + dx],
+            recv_sem=cr_sem.at[g * 4 + dx],
+            device_id=source(g, dx),
             device_id_type=MESH,
         )
 
@@ -216,6 +253,9 @@
         copy.wait()
 
     gain_sum[...] = jnp.zeros_like(gain_sum)
+    on_line = lax.broadcasted_iota(jnp.int32, (32, 128), 0) == lax.broadcasted_iota(
+        jnp.int32, (32, 128), 1
+    )
     order = (0, 1, 4, 2, 5, 3, 6, 7)
 
     def group(i, carry):
@@ -257,22 +297,20 @@
             held = recv[g, :, :, cols].astype(F32)[:, :8]
             gain_sum[:, cols] += jnp.sum(piece * held, axis=0)
         out = jnp.concatenate(halves, axis=1)
-        comb = jnp.broadcast_to(comb, (4, 8, 128))
-        comb = jnp.concatenate([comb, jnp.zeros((4, 8, 128), F32)], axis=1)
+        comb = jnp.where(on_line, comb.reshape(32, 1), 0.0)
+        comb_out[g] = jnp.sum(comb, axis=0, keepdims=True)
         kept = (g == 2) | (g == 3)
         half = (g == 6) | (g == 7)
 
         @pl.when(kept)
         def _():
             for dx in range(NX):
-                hold[(g - 2) * 4 + dx, :, 0:HALF] = out[dx]
-                hold[(g - 2) * 4 + dx, :, HALF:BACK] = comb[dx]
+                hold[(g - 2) * 4 + dx] = out[dx]
 
         @pl.when(jnp.logical_not(kept))
         def _():
             for dx in range(NX):
-                ret[g * 4 + dx, :, 0:HALF] = out[dx].astype(BF16)
-                ret[g * 4 + dx, :, HALF:BACK] = comb[dx].astype(BF16)
+                ret[g * 4 + dx] = out[dx].astype(BF16)
 
         @pl.when(half)
         def _():
@@ -282,17 +320,18 @@
         @pl.when(jnp.logical_not(kept | half))
         def _():
             for dx in range(NX):
-                if dx == 0:
-
-                    @pl.when(g == 0)
-                    def _():
-                        got[0] = ret[0]
-
-                    @pl.when(g > 0)
-                    def _():
-                        giveback(g, 0).start()
-                else:
-                    giveback(g, dx).start()
+                giveback(g, dx).start()
+
+        @pl.when(g == 0)
+        def _():
+            comb_in[0] = comb_out[0]
+
+        @pl.when(g > 0)
+        def _():
+            comb_back(g, 0).start()
+
+        for dx in range(1, NX):
+            comb_back(g, dx).start()
 
         return carry
 
@@ -334,60 +373,36 @@
     for dz in range(1, NZ):
         share_z(dz).start()
 
-    slot, expert, chosen, _ = picks(256, 16)
-    first = lax.rem(slot, 16) < 8
-    low = jnp.where(first, chosen, 0.0).astype(BF16)
-    high = jnp.where(first, 0.0, chosen).astype(BF16)
-    chosen = jnp.where(first, chosen, 0.0)
-
-    for n in [1, 2, 3, 4, 5, 6, 7, 8, 9, 10, 11, 12, 13, 14, 15, 16, 17, 18, 19, 20, 21, 22, 23]:
-        landed(got.at[n], got_sem.at[n])
-
-    spans = [(0, 16, 0), (16, 24, 0)]
-    total = []
-    for side in (low, high):
-        sums = 0.0
-        for lo, hi, at in spans:
-            size = (hi - lo) * 16
-            sums += tn(side[at : at + size], got[lo:hi, :, 0:HALF].reshape(size, HALF))
-        total.append(sums)
-
-    hats = [x_ref[:, c * HALF : (c + 1) * HALF].astype(F32) * rinv for c in range(2)]
-    products = [total[c] * hats[c] for c in range(2)]
-    mean = 0.0
-    for c in range(2):
-        cols = slice(c * HALF, (c + 1) * HALF)
-        mean += jnp.sum(products[c] * g_ref[:, cols], axis=-1, keepdims=True)
-    mean = mean / D
-    for c in range(2):
-        cols = slice(c * HALF, (c + 1) * HALF)
-        scaled_grad = total[c] * g_ref[:, cols]
-        grad = dy_ref[:, cols].astype(F32) + rinv * (scaled_grad - hats[c] * mean)
-        grads[:, cols] = grad.astype(BF16)
-
-    def pass_on():
-        return pltpu.make_async_remote_copy(
-            src_ref=grads,
-            dst_ref=passed_ref,
-            send_sem=pass_sem.at[0],
-            recv_sem=pass_sem.at[1],
-            device_id=ahead,
-            device_id_type=MESH,
-        )
-
-    @pl.when(sec > 0)
-    def _():
-        pass_on().start()
-
+    for copy in pushes:
+        copy.wait()
+
+    later = next_x[...].astype(F32)
+    later_rinv = lax.rsqrt(jnp.mean(later * later, axis=-1, keepdims=True) + EPS)
+    row, _, later_pick, _ = picks(next_ids[...], weights, 256, 16)
+    first = lax.rem(row, 16) < 8
+    low = jnp.where(first, later_pick, 0.0).astype(BF16)
+    high = jnp.where(first, 0.0, later_pick).astype(BF16)
+
+    def comb_landed(n, carry):
+        landed(comb_in.at[n], cr_sem.at[n])
+        return carry
+
+    lax.fori_loop(1, 32, comb_landed, 0)
+    found = comb_in[0:16] + comb_in[16:32]
+    found = jnp.broadcast_to(found, (16, CAP, 128)).reshape(128, 128)
+    spot = lax.rem(lax.broadcasted_iota(jnp.int32, (128, 128), 0), 32)
+    spot = spot == lax.broadcasted_iota(jnp.int32, (128, 128), 1)
+    found = chosen * jnp.sum(jnp.where(spot, found, 0.0), axis=1, keepdims=True)
     line = lax.broadcasted_iota(jnp.int32, (TOP, TOK), 0)
     comb = jnp.zeros((TOP, TOK), F32)
-    found = got[0:16, :, HALF:BACK].astype(F32).reshape(256, 128)[:, 0:TOK]
-    extra = got[16:24, :, HALF:BACK].astype(F32).reshape(128, 128)[:, 0:TOK]
-    found = chosen * jnp.concatenate([found[0:128] + extra, found[128:256]], axis=0)
     for k in range(TOP):
         one = jnp.where(ids[k : k + 1, :] == expert, found, 0.0)
         comb = jnp.where(line == k, jnp.sum(one, axis=0, keepdims=True), comb)
     comb_ref[...] = (comb / weights).astype(BF16)
+
+    for dz in range(1, NZ):
+        share_z(dz).wait()
+    gain_ref[...] = jnp.sum(sum_z[...], axis=0) / g_ref[...]
 
     for d in range(4):
         for dx in range(NX):
@@ -399,25 +414,32 @@
         landed(ret.at[n], ret_sem.at[n])
         return carry
 
-    lax.fori_loop(1, 32, sent, 0)
-    for dz in range(1, NZ):
-        share_z(dz).wait()
-    gain_ref[...] = jnp.sum(sum_z[...], axis=0) / g_ref[...]
-
-    @pl.when(sec > 0)
-    def _():
-        pass_on().wait_send()
-
-    @pl.when(sec < 7)
-    def _():
-        pass_on().wait_recv()
-
-    @pl.when(sec == 7)
-    def _():
-        grads[...] = jnp.zeros_like(grads)
-        clear = pltpu.make_async_copy(grads, passed_ref, pass_sem.at[1])
-        clear.start()
-        clear.wait()
+    lax.fori_loop(0, 32, sent, 0)
+
+    def comb_sent(n, carry):
+        landed(comb_in.at[n], cs_sem.at[n])
+        return carry
+
+    lax.fori_loop(1, 32, comb_sent, 0)
+
+    for n in range(24):
+        landed(got.at[n], got_sem.at[n])
+
+    total = []
+    for side in (low, high):
+        sums = tn(side, got[0:16].reshape(256, HALF))
+        sums += tn(side[0:128], got[16:24].reshape(128, HALF))
+        total.append(sums)
+    hats = [next_x[:, c * HALF : (c + 1) * HALF].astype(F32) * later_rinv for c in range(2)]
+    scaled_grad = [total[c] * next_g[:, c * HALF : (c + 1) * HALF] for c in range(2)]
+    mean = 0.0
+    for c in range(2):
+        mean += jnp.sum(scaled_grad[c] * hats[c], axis=-1, keepdims=True)
+    mean = mean / D
+    for c in range(2):
+        cols = slice(c * HALF, (c + 1) * HALF)
+        grad = next_dy[:, cols].astype(F32) + later_rinv * (scaled_grad[c] - hats[c] * mean)
+        passed_ref[:, cols] = jnp.where(sec == 7, 0.0, grad).astype(BF16)
 
 
 def per_device(layer_input, out_grad, norm_gain, expert_ids, combine, w_gate, w_up, w_down):
@@ -432,27 +454,32 @@
             jax.ShapeDtypeStruct((1, D), F32),
         ),
         in_specs=[hbm] * 8,
-        out_specs=(hbm, vmem, vmem),
+        out_specs=(vmem, vmem, vmem),
         scratch_shapes=[
             pltpu.VMEM((TOK, D), BF16),
             pltpu.VMEM((TOK, D), BF16),
             pltpu.VMEM((1, D), F32),
             pltpu.VMEM((TOP, TOK), jnp.int32),
             pltpu.VMEM((TOP, TOK), BF16),
+            pltpu.VMEM((TOK, D), BF16),
+            pltpu.VMEM((TOK, D), BF16),
+            pltpu.VMEM((1, D), F32),
+            pltpu.VMEM((TOP, TOK), jnp.int32),
             pltpu.VMEM((16, 16, D), BF16),
             pltpu.VMEM((8, NX, 16, D), BF16),
             pltpu.VMEM((6, HID, D), BF16),
-            pltpu.VMEM((32, 16, BACK), BF16),
-            pltpu.VMEM((32, 16, BACK), BF16),
-            pltpu.VMEM((8, 16, BACK), F32),
-            pltpu.VMEM((8, 16, BACK), BF16),
-            pltpu.VMEM((TOK, D), BF16),
+            pltpu.VMEM((32, 16, HALF), BF16),
+            pltpu.VMEM((24, 16, HALF), BF16),
+            pltpu.VMEM((8, 16, HALF), F32),
+            pltpu.VMEM((8, 16, HALF), BF16),
+            pltpu.VMEM((8, 1, 128), F32),
+            pltpu.VMEM((32, 1, 128), F32),
             pltpu.VMEM((8, D), F32),
             pltpu.VMEM((8, 1, D), F32),
             pltpu.VMEM((8, 1, D), F32),
-            dma((5,)), dma((16,)), dma((32,)), dma((16,)), dma((32,)), dma((32,)), dma((8,)),
+            dma((5,)), dma((16,)), dma((32,)), dma((16,)), dma((32,)), dma((24,)), dma((8,)),
             dma((3,)), dma((3,)), dma((3,)),
-            dma((8,)), dma((8,)), dma((8,)), dma((8,)), dma((2,)),
+            dma((4,)), dma((4,)), dma((32,)), dma((32,)), dma((8,)), dma((8,)), dma((8,)), dma((8,)),
         ],
         compiler_params=pltpu.CompilerParams(
             collective_id=0, has_side_effects=True, vmem_limit_bytes=60 * 1024 * 1024

time: 84.3 us -> 82.5 us (0.979)
  the two profiles are of different devices: /device:TPU:152 before, /device:TPU:56 now
where the time goes in v3:
time: 82.5 us; the launch traced here: 82.4 us
  Pallas kernels  78.9 us (96%)
  local copies, waits for them, and re-layouts  2.86 us (3%)
    pallas_call x1, Pallas kernels, per_device(): pl.pallas_call(kernel, out_shape=(jax.ShapeDtypeStruct((TOK, D), BF16), j...  78.9 us
    unnamed x7, local copies, waits for them, and re-layouts  2.86 us

profile of v3, /device:TPU:56, one launch (start us, length us, event | category | flops | bytes accessed | tf_op | source)
XLA Modules:
  0.0 82.4 jit_solution(13804560129197699823)
XLA Ops:
  0.6 78.9 %shard_map.103 = (bf16[64,2048]{1,0:T(8,128)(2,1)}, bf16[8,64]{1,0:T(8,128)(2,1)}, f32[1,2048]{1,0:T(1,128)}) custom-call(bf16[64,2048]{1,0:T(8,128)(2,1)} %bitcast.18, bf16[64,2048]{1,0:T(8,128)(2,1)} %bitcast.19, f32[1,2048]{1,0:T(1,128)} %g_hbm.1, s32[8,64]{1,0:T(8,128)} %bitcast.21, bf16[8,64]{1,0:T(8,128)(2,1)} %bitcast.22, bf16[192,2048]{1,0:T(8,128)(2,1)} %bitcast.15, ...), custom_call_target="tpu_custom_call" | custom-call | tf_op jit(solution)/shard_map/pallas_call | solution.py:449
  79.5 0.0 copy-start.1
  79.5 0.0 copy-start
  79.5 1.7 %copy.14 = bf16[1,64,2048]{2,1,0:T(8,128)(2,1)} copy(bf16[1,64,2048]{2,1,0:T(8,128)(2,1)} %bitcast.20) | data formatting | bytes 524288
  81.2 0.0 copy-done.1
  81.2 0.6 copy.15
  81.8 0.0 copy-done
  81.8 0.6 copy.16
Async XLA Ops:
  79.5 1.7 %copy-start.1 = (bf16[8,64]{1,0:T(8,128)(2,1)S(1)}, bf16[8,64]{1,0:T(8,128)(2,1)}, u32[]{:S(2)}) copy-start(bf16[8,64]{1,0:T(8,128)(2,1)} %get-tuple-element.7) | copy-start | bytes 3076
  79.5 2.3 %copy-start = (f32[1,2048]{1,0:T(1,128)S(1)}, f32[1,2048]{1,0:T(1,128)}, u32[]{:S(2)}) copy-start(f32[1,2048]{1,0:T(1,128)} %get-tuple-element.14) | copy-start | bytes 24580

commit v4 on v3

--- a/solution.py
+++ b/solution.py
@@ -168,7 +168,7 @@
 
     hand_on(0, 0).start()
     swaps = [weight_swap(n, ref) for n, ref in enumerate((wg_ref, wu_ref, wd_ref))]
-    for d in range(4):
+    for d in (0, 1, 2, 3):
         for dx in range(NX):
             if (d, dx) != (0, 0):
                 dispatch(d, dx).start()
@@ -256,7 +256,7 @@
     on_line = lax.broadcasted_iota(jnp.int32, (32, 128), 0) == lax.broadcasted_iota(
         jnp.int32, (32, 128), 1
     )
-    order = (0, 1, 4, 2, 5, 3, 6, 7)
+    order = (0, 4, 1, 5, 2, 3, 6, 7)
 
     def group(i, carry):
         g = jnp.int32(order[0])
@@ -267,7 +267,7 @@
         def _():
             forward(2)
 
-        @pl.when(i == 2)
+        @pl.when(i == 3)
         def _():
             forward(3)
 

time: 82.5 us -> 80.3 us (0.973)
  Pallas kernels: 78.9 us -> 76.1 us
    pallas_call x1, Pallas kernels: 78.9 us -> 76.1 us  [per_device(): pl.pallas_call(kernel, out_shape=(jax.ShapeDtypeStruct((TOK, D), BF16), j...]
where the time goes in v4:
time: 80.3 us; the launch traced here: 79.6 us
  Pallas kernels  76.1 us (95%)
  local copies, waits for them, and re-layouts  2.86 us (4%)
    pallas_call x1, Pallas kernels, per_device(): pl.pallas_call(kernel, out_shape=(jax.ShapeDtypeStruct((TOK, D), BF16), j...  76.1 us
    unnamed x7, local copies, waits for them, and re-layouts  2.86 us

profile of v4, /device:TPU:56, one launch (start us, length us, event | category | flops | bytes accessed | tf_op | source)
XLA Modules:
  0.0 79.6 jit_solution(8206485598680067780)
XLA Ops:
  0.6 76.1 %shard_map.103 = (bf16[64,2048]{1,0:T(8,128)(2,1)}, bf16[8,64]{1,0:T(8,128)(2,1)}, f32[1,2048]{1,0:T(1,128)}) custom-call(bf16[64,2048]{1,0:T(8,128)(2,1)} %bitcast.18, bf16[64,2048]{1,0:T(8,128)(2,1)} %bitcast.19, f32[1,2048]{1,0:T(1,128)} %g_hbm.1, s32[8,64]{1,0:T(8,128)} %bitcast.21, bf16[8,64]{1,0:T(8,128)(2,1)} %bitcast.22, bf16[192,2048]{1,0:T(8,128)(2,1)} %bitcast.15, ...), custom_call_target="tpu_custom_call" | custom-call | tf_op jit(solution)/shard_map/pallas_call | solution.py:449
  76.8 0.0 copy-start.1
  76.8 0.0 copy-start
  76.8 1.7 %copy.14 = bf16[1,64,2048]{2,1,0:T(8,128)(2,1)} copy(bf16[1,64,2048]{2,1,0:T(8,128)(2,1)} %bitcast.20) | data formatting | bytes 524288
  78.4 0.0 copy-done.1
  78.5 0.6 copy.15
  79.0 0.0 copy-done
  79.0 0.6 copy.16
Async XLA Ops:
  76.8 1.7 %copy-start.1 = (bf16[8,64]{1,0:T(8,128)(2,1)S(1)}, bf16[8,64]{1,0:T(8,128)(2,1)}, u32[]{:S(2)}) copy-start(bf16[8,64]{1,0:T(8,128)(2,1)} %get-tuple-element.7) | copy-start | bytes 3076
  76.8 2.3 %copy-start = (f32[1,2048]{1,0:T(1,128)S(1)}, f32[1,2048]{1,0:T(1,128)}, u32[]{:S(2)}) copy-start(f32[1,2048]{1,0:T(1,128)} %get-tuple-element.14) | copy-start | bytes 24580
